TPU v7x, 32 devices: a whole 2x2x4 slice. The times are simulated.
32 devices in a mesh: groups: 2 (over y), qrow: 4 (over z), db: 2 (over x), rep: 2 (over core).
Axes of the slice: x: 2, y: 2, z: 4, core: 2. Of those that a mesh axis runs over, the one named last changes fastest.
Arguments:
- queries: bfloat16 [8, 8, 8, 1024], P(('groups', 'qrow')), parts along dimension 0, may hold values from -6 to 6
- db_maps: bfloat16 [8, 256, 1024], P(('groups', 'db', 'rep')), parts along dimension 0, may hold values from -6 to 6
- round_owner: int32 [6], P('groups'), parts along dimension 0, may hold values from 0 to 3, as said below
- conv1_weight: bfloat16 [16, 3, 3, 3, 3], replicated, may hold values from -2 to 2
- conv1_bias: float32 [16], replicated, may hold values from -0.2 to 0.2
- conv2_weight: bfloat16 [16, 3, 3, 3, 3], replicated, may hold values from -0.5 to 0.5
- conv2_bias: float32 [1], replicated, may hold values from -0.3 to 0.3
Outputs:
- match_scores: float32 [3, 8, 8, 8, 256], P(None, ('groups', 'db', 'rep'), 'qrow'), parts along dimension 1
There are 2 independent parts, one for each index of `groups`. A program takes and returns all parts, laid end to end along the dimension named above; an argument that names none is the same for every part. Nothing has to cross between parts.
Inputs may be any that keep to these rules, and one draw needn't show every extreme that they name: Round r verifies query map round_owner[r]; the rounds verify distinct maps.
All inputs are finite; a program needn't handle non-finite values.
Results may differ from a plain program's by a relative error of at most 0.0049.
Values may be sent and summed in bfloat16 or wider, within the bound.
A program may use at most 64 MiB of HBM per device.

v0:
```python
import functools
import math

import jax
import jax.numpy as jnp
from jax import lax
from jax.experimental import pallas as pl
from jax.experimental.pallas import tpu as pltpu
from jax.sharding import PartitionSpec as P

epsilon = 1e-05
TAPS = 9
SLOTS = 10
LANE_STEP = 256
STRIDE = 32


def tap_row(a, b, c, d):
    return d * STRIDE + (a * 3 + b) * 3 + c


def tap_matrix(weight_ref, spread):
    spread[...] = jnp.zeros_like(spread)
    groups, inner, channels = weight_ref.shape
    values = weight_ref[...].astype(jnp.float32)
    for d in range(inner):
        spread[pl.ds(d * STRIDE, groups), pl.ds(0, channels)] = values[:, d, :]
    return spread[...][:, :channels].astype(jnp.bfloat16)


def banded(masks, parts):
    value = jnp.zeros(masks[0].shape, jnp.float32)
    for mask, part in zip(masks, parts):
        value = jnp.where(mask, jnp.broadcast_to(part, mask.shape), value)
    return value


def first_matrix(taps, width, chosen_ref):
    rows, channels = taps.shape
    block = SLOTS * width
    lane = lax.broadcasted_iota(jnp.int32, (1, LANE_STEP), 1)
    a = sum((lane >= k * block).astype(jnp.int32) for k in (1, 2))
    offset = lane - a * block
    tap = sum((offset >= k * width).astype(jnp.int32) for k in range(1, SLOTS))
    c = (tap >= 3).astype(jnp.int32) + (tap >= 6).astype(jnp.int32)
    d = tap - 3 * c
    valid = (tap < TAPS) & (lane < 3 * block)
    base = jnp.where(valid, d * STRIDE + a * 9 + c, -rows)
    row = lax.broadcasted_iota(jnp.int32, (rows, LANE_STEP), 0)
    for b in range(3):
        pick = jnp.where(row == base + 3 * b, 1.0, 0.0).astype(jnp.bfloat16)
        chosen_ref[b] = lax.dot_general(
            taps, pick, (((0,), (0,)), ((), ())), preferred_element_type=jnp.float32
        )
    band = offset - tap * width - lax.broadcasted_iota(jnp.int32, (width, LANE_STEP), 0) + 1
    masks = [band == b for b in range(3)]
    return jnp.concatenate(
        [
            banded(masks, [chosen_ref[b, pl.ds(o, 1), :] for b in range(3)])
            for o in range(channels)
        ],
        axis=0,
    ).astype(jnp.bfloat16)[:, : 3 * block]


def second_matrix(taps, width, wide_ref):
    channels = taps.shape[1]
    lanes = channels * width
    lane = lax.broadcasted_iota(jnp.int32, (channels, lanes), 1)
    start = lax.broadcasted_iota(jnp.int32, (channels, lanes), 0) * width
    repeat = jnp.where((lane >= start) & (lane < start + width), 1.0, 0.0).astype(jnp.bfloat16)
    wide_ref[...] = jnp.dot(taps, repeat, preferred_element_type=jnp.float32)
    channel = sum(
        (lax.broadcasted_iota(jnp.int32, (1, lanes), 1) >= k * width).astype(jnp.int32)
        for k in range(1, channels)
    )
    column = lax.broadcasted_iota(jnp.int32, (1, lanes), 1) - channel * width
    band = column - lax.broadcasted_iota(jnp.int32, (width, lanes), 0) + 1
    masks = [band == b for b in range(3)]
    return jnp.concatenate(
        [
            banded(masks, [wide_ref[pl.ds(tap_row(a, b, c, d), 1), :] for b in range(3)])
            for a in range(3)
            for c in range(3)
            for d in range(3)
        ],
        axis=0,
    ).astype(jnp.bfloat16)


def kernel(
    count,
    width,
    side,
    owner_hbm,
    bias1_hbm,
    bias2_hbm,
    query_hbm,
    map_hbm,
    weight1_hbm,
    weight2_hbm,
    out_ref,
    owner_ref,
    bias1_ref,
    bias2_ref,
    query_ref,
    map_ref,
    weight1_ref,
    weight2_ref,
    spread1,
    spread2,
    chosen,
    wide,
    shifted,
    result,
    received,
    load_sem,
    send_sem,
    recv_sem,
):
    loads = [
        pltpu.make_async_copy(source, target, load_sem.at[index])
        for index, (source, target) in enumerate(
            (
                (weight1_hbm, weight1_ref),
                (weight2_hbm, weight2_ref),
                (map_hbm, map_ref),
                (query_hbm, query_ref),
                (bias1_hbm, bias1_ref),
                (bias2_hbm, bias2_ref),
                (owner_hbm, owner_ref),
            )
        )
    ]
    for load in loads:
        load.start()
    me = lax.axis_index("qrow")
    barrier = pltpu.get_barrier_semaphore()
    for step in range(1, count):
        pl.semaphore_signal(
            barrier,
            inc=1,
            device_id={"qrow": lax.rem(me + step, count)},
            device_id_type=pl.DeviceIdType.MESH,
        )

    positions = map_ref.shape[0]
    rows = query_ref.shape[0] // width
    channels = weight1_ref.shape[2]
    block = SLOTS * width
    size = TAPS * width

    loads[0].wait()
    loads[1].wait()
    matrix1 = first_matrix(tap_matrix(weight1_ref, spread1), width, chosen)
    matrix2 = second_matrix(tap_matrix(weight2_ref, spread2), width, wide)
    for load in loads[2:]:
        load.wait()

    corr = lax.dot_general(
        query_ref[...],
        map_ref[...],
        (((1,), (1,)), ((), ())),
        preferred_element_type=jnp.float32,
    ) * (1.0 / math.sqrt(query_ref.shape[1]))
    scores = jnp.maximum(corr, 0.0)
    col_scale = 1.0 / (jnp.max(scores, axis=0, keepdims=True) + epsilon)
    row_scale = 1.0 / (jnp.max(scores, axis=1, keepdims=True) + epsilon)
    mutual = scores * (scores * col_scale) * (scores * row_scale)

    lane = lax.broadcasted_iota(jnp.int32, (1, positions), 1)
    column = lane & (side - 1)

    def inner(value, d):
        if d == 1:
            return value
        moved = pltpu.roll(value, (1 - d) % positions, 1)
        return jnp.where(column == (0 if d == 0 else side - 1), 0.0, moved)

    def outer(value, c):
        if c == 1:
            return value
        moved = pltpu.roll(value, ((1 - c) * side) % positions, 1)
        edge = lane < side if c == 0 else lane >= positions - side
        return jnp.where(edge, 0.0, moved)

    along = [inner(mutual, d) for d in range(3)]
    taps = [outer(along[d], c) for c in range(3) for d in range(3)]
    blank = jnp.zeros((block, positions), jnp.bfloat16)
    shifted[pl.ds(0, block), :] = blank
    shifted[pl.ds((rows + 1) * block, block), :] = blank
    gap = jnp.zeros((width, positions), jnp.float32)
    for i in range(rows):
        shifted[pl.ds((i + 1) * block, block), :] = jnp.concatenate(
            [tap[i * width : (i + 1) * width] for tap in taps] + [gap], axis=0
        ).astype(jnp.bfloat16)

    bias1 = jnp.concatenate(
        [jnp.full((width, positions), bias1_ref[o], jnp.float32) for o in range(channels)], axis=0
    )
    mixed = []
    for i in range(rows):
        hidden = jnp.dot(
            matrix1, shifted[pl.ds(i * block, 3 * block), :], preferred_element_type=jnp.float32
        )
        hidden = jnp.maximum(hidden + bias1, 0.0).astype(jnp.bfloat16)
        mixed.append(jnp.dot(matrix2, hidden, preferred_element_type=jnp.float32))

    each = rows // count
    for target in range(count):
        totals = []
        for i in range(target * each, (target + 1) * each):
            summed = mixed[i][size : 2 * size]
            if i > 0:
                summed = summed + mixed[i - 1][:size]
            if i < rows - 1:
                summed = summed + mixed[i + 1][2 * size :]
            total = None
            for c in range(3):
                row = None
                for d in range(3):
                    tap = (c * 3 + d) * width
                    term = inner(summed[tap : tap + width], d)
                    row = term if row is None else row + term
                row = outer(row, c)
                total = row if total is None else total + row
            totals.append(jnp.maximum(total + bias2_ref[0], 0.0))
        result[target] = jnp.concatenate(totals, axis=0)

    pl.semaphore_wait(barrier, count - 1)

    def transfer(source, target):
        return pltpu.make_async_remote_copy(
            src_ref=result.at[target],
            dst_ref=received.at[source],
            send_sem=send_sem.at[target],
            recv_sem=recv_sem.at[source],
            device_id={"qrow": target},
            device_id_type=pl.DeviceIdType.MESH,
        )

    for step in range(1, count):
        transfer(me, lax.rem(me + step, count)).start()
    received[me] = result[me]
    for step in range(1, count):
        transfer(lax.rem(me + step, count), me).wait_recv()
    for r in range(out_ref.shape[0]):
        out_ref[r] = received[owner_ref[r]]
    for step in range(1, count):
        transfer(me, lax.rem(me + step, count)).wait_send()


def on_device(count, queries, db_maps, round_owner, conv1_weight, conv1_bias, conv2_weight, conv2_bias):
    maps, rows, width, depth = queries.shape
    positions = db_maps.shape[1]
    channels = conv1_weight.shape[0]
    side = math.isqrt(positions)
    each = rows // count
    block = SLOTS * width
    rounds = round_owner.shape[0]

    def taps_first(weight):
        return jnp.transpose(weight, (1, 2, 3, 4, 0)).reshape(27, 3, channels)

    result = pl.pallas_call(
        functools.partial(kernel, count, width, side),
        out_shape=jax.ShapeDtypeStruct((rounds, each * width, positions), jnp.float32),
        in_specs=[pl.BlockSpec(memory_space=pltpu.HBM)] * 7,
        out_specs=pl.BlockSpec(memory_space=pltpu.VMEM),
        scratch_shapes=[
            pltpu.SMEM((rounds,), jnp.int32),
            pltpu.SMEM((channels,), jnp.float32),
            pltpu.SMEM((1,), jnp.float32),
            pltpu.VMEM((rows * width, depth), jnp.bfloat16),
            pltpu.VMEM((positions, depth), jnp.bfloat16),
            pltpu.VMEM((27, 3, channels), jnp.bfloat16),
            pltpu.VMEM((27, 3, channels), jnp.bfloat16),
            pltpu.VMEM((3 * STRIDE, 128), jnp.float32),
            pltpu.VMEM((3 * STRIDE, 128), jnp.float32),
            pltpu.VMEM((3, channels, LANE_STEP), jnp.float32),
            pltpu.VMEM((3 * STRIDE, channels * width), jnp.float32),
            pltpu.VMEM(((rows + 2) * block, positions), jnp.bfloat16),
            pltpu.VMEM((count, each * width, positions), jnp.float32),
            pltpu.VMEM((count, each * width, positions), jnp.float32),
            pltpu.SemaphoreType.DMA((7,)),
            pltpu.SemaphoreType.DMA((count,)),
            pltpu.SemaphoreType.DMA((count,)),
        ],
        compiler_params=pltpu.CompilerParams(
            collective_id=0, has_side_effects=True, vmem_limit_bytes=60 * 1024 * 1024
        ),
        name="verify",
    )(
        round_owner,
        conv1_bias,
        conv2_bias,
        queries.reshape(maps * rows * width, depth),
        db_maps.reshape(positions, depth),
        taps_first(conv1_weight),
        taps_first(conv2_weight),
    )
    return result.reshape(rounds, 1, each, width, positions)


def solution(mesh):
    placed = (
        P(("groups", "qrow"), None, None, None),
        P(("groups", "db", "rep"), None, None),
        P("groups"),
        P(),
        P(),
        P(),
        P(),
    )
    return jax.shard_map(
        functools.partial(on_device, mesh.shape["qrow"]),
        mesh=mesh,
        in_specs=placed,
        out_specs=P(None, ("groups", "db", "rep"), "qrow", None, None),
        check_vma=False,
    )
```

profile of v0, /device:TPU:0, one launch (start us, length us, event | category | flops | bytes accessed | tf_op | source)
XLA Modules:
  0.0 12.8 jit_solution(2696725023426959170)
XLA Ops:
  0.7 10.7 %verify.1 = f32[3,16,256]{2,1,0:T(8,128)} custom-call(s32[3]{0:T(128)} %owner_hbm.1, f32[16]{0:T(128)} %bias1_hbm.1, f32[1]{0:T(128)S(6)} %copy.10.bias2_hbm, bf16[64,1024]{1,0:T(8,128)(2,1)} %bitcast.13, bf16[256,1024]{1,0:T(8,128)(2,1)} %bitcast.11, bf16[27,3,16]{2,1,0:T(4,128)(2,1)} %bitcast.14, bf16[27,3,16]{2,1,0:T(4,128)(2,1)} %bitcast.15), custom_call_target="tpu_custom_call" | custom-call | tf_op jit(solution)/shard_map/verify/pallas_call | solution.py:265
  11.4 1.4 %copy.11 = f32[3,1,2,8,256]{4,3,2,1,0:T(8,128)} copy(f32[3,1,2,8,256]{4,3,2,1,0:T(8,128)} %bitcast.12) | data formatting | bytes 98304
where the time goes:
time: 13 us; the launch traced here: 12.8 us
  Pallas kernels  10.7 us (82%)
  local copies, waits for them, and re-layouts  1.42 us (11%)
  between operations  0.66 us (5%)
    pallas_call x1, Pallas kernels, on_device(): pl.pallas_call(functools.partial(kernel, count, width, side), out_shape=j...  10.7 us
    unnamed x1, local copies, waits for them, and re-layouts  1.42 us

commit v1 on v0

--- a/solution.py
+++ b/solution.py
@@ -12,20 +12,18 @@
 TAPS = 9
 SLOTS = 10
 LANE_STEP = 256
-STRIDE = 32
+STRIDE = 8
+GROUPS = 28
 
 
 def tap_row(a, b, c, d):
-    return d * STRIDE + (a * 3 + b) * 3 + c
+    return ((a * 3 + b) * 3 + c) * STRIDE + d
 
 
 def tap_matrix(weight_ref, spread):
-    spread[...] = jnp.zeros_like(spread)
     groups, inner, channels = weight_ref.shape
-    values = weight_ref[...].astype(jnp.float32)
-    for d in range(inner):
-        spread[pl.ds(d * STRIDE, groups), pl.ds(0, channels)] = values[:, d, :]
-    return spread[...][:, :channels].astype(jnp.bfloat16)
+    spread[pl.ds(0, groups), pl.ds(0, inner), :] = weight_ref[...].astype(jnp.float32)
+    return spread[...].reshape(GROUPS * STRIDE, channels).astype(jnp.bfloat16)
 
 
 def banded(masks, parts):
@@ -35,8 +33,8 @@
     return value
 
 
-def first_matrix(taps, width, chosen_ref):
-    rows, channels = taps.shape
+def fill_picks(width, pick_ref):
+    rows = GROUPS * STRIDE
     block = SLOTS * width
     lane = lax.broadcasted_iota(jnp.int32, (1, LANE_STEP), 1)
     a = sum((lane >= k * block).astype(jnp.int32) for k in (1, 2))
@@ -45,22 +43,26 @@
     c = (tap >= 3).astype(jnp.int32) + (tap >= 6).astype(jnp.int32)
     d = tap - 3 * c
     valid = (tap < TAPS) & (lane < 3 * block)
-    base = jnp.where(valid, d * STRIDE + a * 9 + c, -rows)
+    base = jnp.where(valid, tap_row(a, 0, c, d), -2 * rows)
     row = lax.broadcasted_iota(jnp.int32, (rows, LANE_STEP), 0)
     for b in range(3):
-        pick = jnp.where(row == base + 3 * b, 1.0, 0.0).astype(jnp.bfloat16)
+        pick_ref[b] = jnp.where(row == base + tap_row(0, b, 0, 0), 1.0, 0.0).astype(jnp.bfloat16)
+    return offset - tap * width - lax.broadcasted_iota(jnp.int32, (width, LANE_STEP), 0) + 1
+
+
+def first_matrix(taps, width, pick_ref, band, chosen_ref):
+    for b in range(3):
         chosen_ref[b] = lax.dot_general(
-            taps, pick, (((0,), (0,)), ((), ())), preferred_element_type=jnp.float32
-        )
-    band = offset - tap * width - lax.broadcasted_iota(jnp.int32, (width, LANE_STEP), 0) + 1
+            taps, pick_ref[b], (((0,), (0,)), ((), ())), preferred_element_type=jnp.float32
+        )
     masks = [band == b for b in range(3)]
     return jnp.concatenate(
         [
             banded(masks, [chosen_ref[b, pl.ds(o, 1), :] for b in range(3)])
-            for o in range(channels)
+            for o in range(taps.shape[1])
         ],
         axis=0,
-    ).astype(jnp.bfloat16)[:, : 3 * block]
+    ).astype(jnp.bfloat16)[:, : 3 * SLOTS * width]
 
 
 def second_matrix(taps, width, wide_ref):
@@ -109,6 +111,7 @@
     weight2_ref,
     spread1,
     spread2,
+    pick,
     chosen,
     wide,
     shifted,
@@ -150,12 +153,17 @@
     block = SLOTS * width
     size = TAPS * width
 
-    loads[0].wait()
-    loads[1].wait()
-    matrix1 = first_matrix(tap_matrix(weight1_ref, spread1), width, chosen)
+    band = fill_picks(width, pick)
+    for spread in (spread1, spread2):
+        spread[...] = jnp.zeros_like(spread)
+    blank = jnp.zeros((block, positions), jnp.bfloat16)
+    shifted[pl.ds(0, block), :] = blank
+    shifted[pl.ds((rows + 1) * block, block), :] = blank
+    for load in loads:
+        load.wait()
+
+    matrix1 = first_matrix(tap_matrix(weight1_ref, spread1), width, pick, band, chosen)
     matrix2 = second_matrix(tap_matrix(weight2_ref, spread2), width, wide)
-    for load in loads[2:]:
-        load.wait()
 
     corr = lax.dot_general(
         query_ref[...],
@@ -186,9 +194,6 @@
 
     along = [inner(mutual, d) for d in range(3)]
     taps = [outer(along[d], c) for c in range(3) for d in range(3)]
-    blank = jnp.zeros((block, positions), jnp.bfloat16)
-    shifted[pl.ds(0, block), :] = blank
-    shifted[pl.ds((rows + 1) * block, block), :] = blank
     gap = jnp.zeros((width, positions), jnp.float32)
     for i in range(rows):
         shifted[pl.ds((i + 1) * block, block), :] = jnp.concatenate(
@@ -225,7 +230,7 @@
                 row = outer(row, c)
                 total = row if total is None else total + row
             totals.append(jnp.maximum(total + bias2_ref[0], 0.0))
-        result[target] = jnp.concatenate(totals, axis=0)
+        result[target] = jnp.concatenate(totals, axis=0).astype(jnp.bfloat16)
 
     pl.semaphore_wait(barrier, count - 1)
 
@@ -245,7 +250,7 @@
     for step in range(1, count):
         transfer(lax.rem(me + step, count), me).wait_recv()
     for r in range(out_ref.shape[0]):
-        out_ref[r] = received[owner_ref[r]]
+        out_ref[r] = received[owner_ref[r]].astype(jnp.float32)
     for step in range(1, count):
         transfer(me, lax.rem(me + step, count)).wait_send()
 
@@ -275,13 +280,14 @@
             pltpu.VMEM((positions, depth), jnp.bfloat16),
             pltpu.VMEM((27, 3, channels), jnp.bfloat16),
             pltpu.VMEM((27, 3, channels), jnp.bfloat16),
-            pltpu.VMEM((3 * STRIDE, 128), jnp.float32),
-            pltpu.VMEM((3 * STRIDE, 128), jnp.float32),
+            pltpu.VMEM((GROUPS, STRIDE, channels), jnp.float32),
+            pltpu.VMEM((GROUPS, STRIDE, channels), jnp.float32),
+            pltpu.VMEM((3, GROUPS * STRIDE, LANE_STEP), jnp.bfloat16),
             pltpu.VMEM((3, channels, LANE_STEP), jnp.float32),
-            pltpu.VMEM((3 * STRIDE, channels * width), jnp.float32),
+            pltpu.VMEM((GROUPS * STRIDE, channels * width), jnp.float32),
             pltpu.VMEM(((rows + 2) * block, positions), jnp.bfloat16),
-            pltpu.VMEM((count, each * width, positions), jnp.float32),
-            pltpu.VMEM((count, each * width, positions), jnp.float32),
+            pltpu.VMEM((count, each * width, positions), jnp.bfloat16),
+            pltpu.VMEM((count, each * width, positions), jnp.bfloat16),
             pltpu.SemaphoreType.DMA((7,)),
             pltpu.SemaphoreType.DMA((count,)),
             pltpu.SemaphoreType.DMA((count,)),

time: 13 us -> 13.1 us (level)
  no operation moved by 1% of the time
where the time goes in v1:
time: 13.1 us; the launch traced here: 12.9 us
  Pallas kernels  10.8 us (82%)
  local copies, waits for them, and re-layouts  1.42 us (11%)
  between operations  0.66 us (5%)
    pallas_call x1, Pallas kernels, on_device(): pl.pallas_call(functools.partial(kernel, count, width, side), out_shape=j...  10.8 us
    unnamed x1, local copies, waits for them, and re-layouts  1.42 us

profile of v1, /device:TPU:0, one launch (start us, length us, event | category | flops | bytes accessed | tf_op | source)
XLA Modules:
  0.0 12.9 jit_solution(5933792073583213965)
XLA Ops:
  0.7 10.8 %verify.1 = f32[3,16,256]{2,1,0:T(8,128)} custom-call(s32[3]{0:T(128)} %owner_hbm.1, f32[16]{0:T(128)} %bias1_hbm.1, f32[1]{0:T(128)S(6)} %copy.10.bias2_hbm, bf16[64,1024]{1,0:T(8,128)(2,1)} %bitcast.13, bf16[256,1024]{1,0:T(8,128)(2,1)} %bitcast.11, bf16[27,3,16]{2,1,0:T(4,128)(2,1)} %bitcast.14, bf16[27,3,16]{2,1,0:T(4,128)(2,1)} %bitcast.15), custom_call_target="tpu_custom_call" | custom-call | tf_op jit(solution)/shard_map/verify/pallas_call | solution.py:270
  11.5 1.4 %copy.11 = f32[3,1,2,8,256]{4,3,2,1,0:T(8,128)} copy(f32[3,1,2,8,256]{4,3,2,1,0:T(8,128)} %bitcast.12) | data formatting | bytes 98304

commit v2 on v1

--- a/solution.py
+++ b/solution.py
@@ -96,7 +96,6 @@
     side,
     owner_hbm,
     bias1_hbm,
-    bias2_hbm,
     query_hbm,
     map_hbm,
     weight1_hbm,
@@ -104,7 +103,6 @@
     out_ref,
     owner_ref,
     bias1_ref,
-    bias2_ref,
     query_ref,
     map_ref,
     weight1_ref,
@@ -130,7 +128,6 @@
                 (map_hbm, map_ref),
                 (query_hbm, query_ref),
                 (bias1_hbm, bias1_ref),
-                (bias2_hbm, bias2_ref),
                 (owner_hbm, owner_ref),
             )
         )
@@ -229,8 +226,8 @@
                     row = term if row is None else row + term
                 row = outer(row, c)
                 total = row if total is None else total + row
-            totals.append(jnp.maximum(total + bias2_ref[0], 0.0))
-        result[target] = jnp.concatenate(totals, axis=0).astype(jnp.bfloat16)
+            totals.append(total)
+        result[target] = jnp.concatenate(totals, axis=0)
 
     pl.semaphore_wait(barrier, count - 1)
 
@@ -250,7 +247,7 @@
     for step in range(1, count):
         transfer(lax.rem(me + step, count), me).wait_recv()
     for r in range(out_ref.shape[0]):
-        out_ref[r] = received[owner_ref[r]].astype(jnp.float32)
+        out_ref[r] = received[owner_ref[r]]
     for step in range(1, count):
         transfer(me, lax.rem(me + step, count)).wait_send()
 
@@ -269,13 +266,12 @@
 
     result = pl.pallas_call(
         functools.partial(kernel, count, width, side),
-        out_shape=jax.ShapeDtypeStruct((rounds, each * width, positions), jnp.float32),
-        in_specs=[pl.BlockSpec(memory_space=pltpu.HBM)] * 7,
+        out_shape=pltpu.VMEM((rounds, each * width, positions), jnp.float32),
+        in_specs=[pl.BlockSpec(memory_space=pltpu.HBM)] * 6,
         out_specs=pl.BlockSpec(memory_space=pltpu.VMEM),
         scratch_shapes=[
             pltpu.SMEM((rounds,), jnp.int32),
             pltpu.SMEM((channels,), jnp.float32),
-            pltpu.SMEM((1,), jnp.float32),
             pltpu.VMEM((rows * width, depth), jnp.bfloat16),
             pltpu.VMEM((positions, depth), jnp.bfloat16),
             pltpu.VMEM((27, 3, channels), jnp.bfloat16),
@@ -286,9 +282,9 @@
             pltpu.VMEM((3, channels, LANE_STEP), jnp.float32),
             pltpu.VMEM((GROUPS * STRIDE, channels * width), jnp.float32),
             pltpu.VMEM(((rows + 2) * block, positions), jnp.bfloat16),
-            pltpu.VMEM((count, each * width, positions), jnp.bfloat16),
-            pltpu.VMEM((count, each * width, positions), jnp.bfloat16),
-            pltpu.SemaphoreType.DMA((7,)),
+            pltpu.VMEM((count, each * width, positions), jnp.float32),
+            pltpu.VMEM((count, each * width, positions), jnp.float32),
+            pltpu.SemaphoreType.DMA((6,)),
             pltpu.SemaphoreType.DMA((count,)),
             pltpu.SemaphoreType.DMA((count,)),
         ],
@@ -299,13 +295,12 @@
     )(
         round_owner,
         conv1_bias,
-        conv2_bias,
         queries.reshape(maps * rows * width, depth),
         db_maps.reshape(positions, depth),
         taps_first(conv1_weight),
         taps_first(conv2_weight),
     )
-    return result.reshape(rounds, 1, each, width, positions)
+    return jnp.maximum(result + conv2_bias[0], 0.0).reshape(rounds, 1, each, width, positions)
 
 
 def solution(mesh):

time: 13.1 us -> 11.7 us (0.89)
  local copies, waits for them, and re-layouts: 1.42 us -> 0 us
  other arithmetic: 0 us -> 0.63 us
  Pallas kernels: 10.8 us -> 10.3 us
    unnamed x1 -> x0, local copies, waits for them, and re-layouts: 1.42 us -> none
    reshape x0 -> x1, other arithmetic: none -> 0.63 us  [on_device(): jnp.maximum(result + conv2_bias[0], 0.0)]
    pallas_call x1, Pallas kernels: 10.8 us -> 10.3 us  [on_device(): pl.pallas_call(functools.partial(kernel, count, width, side), out_shape=p...]
where the time goes in v2:
time: 11.7 us; the launch traced here: 11.6 us
  Pallas kernels  10.3 us (88%)
  between operations  0.66 us (6%)
  other arithmetic  0.63 us (5%)
    pallas_call x1, Pallas kernels, on_device(): pl.pallas_call(functools.partial(kernel, count, width, side), out_shape=p...  10.3 us
    reshape x1, other arithmetic, on_device(): jnp.maximum(result + conv2_bias[0], 0.0)  0.63 us

profile of v2, /device:TPU:0, one launch (start us, length us, event | category | flops | bytes accessed | tf_op | source)
XLA Modules:
  0.0 11.6 jit_solution(4946216369930294719)
XLA Ops:
  0.7 10.3 %verify.1 = f32[3,16,256]{2,1,0:T(8,128)S(1)} custom-call(s32[3]{0:T(128)} %owner_hbm.1, f32[16]{0:T(128)} %bias1_hbm.1, bf16[64,1024]{1,0:T(8,128)(2,1)} %bitcast.15, bf16[256,1024]{1,0:T(8,128)(2,1)} %bitcast.14, bf16[27,3,16]{2,1,0:T(4,128)(2,1)} %bitcast.16, bf16[27,3,16]{2,1,0:T(4,128)(2,1)} %bitcast.17), custom_call_target="tpu_custom_call" | custom-call | tf_op jit(solution)/shard_map/verify/pallas_call | solution.py:267
  10.9 0.6 %maximum_bitcast_fusion = f32[3,1,2,8,256]{4,3,2,1,0:T(8,128)} fusion(f32[3,16,256]{2,1,0:T(8,128)S(1)} %verify.1, f32[]{:T(128)} %bitcast.13), kind=kLoop, calls=%fused_computation | loop fusion | flops 24576 | bytes 98308 | tf_op jit(solution)/shard_map/reshape | solution.py:303

commit v3 on v2

--- a/solution.py
+++ b/solution.py
@@ -200,16 +200,26 @@
     bias1 = jnp.concatenate(
         [jnp.full((width, positions), bias1_ref[o], jnp.float32) for o in range(channels)], axis=0
     )
+    def transfer(source, target):
+        return pltpu.make_async_remote_copy(
+            src_ref=result.at[target],
+            dst_ref=received.at[source],
+            send_sem=send_sem.at[target],
+            recv_sem=recv_sem.at[source],
+            device_id={"qrow": target},
+            device_id_type=pl.DeviceIdType.MESH,
+        )
+
+    pl.semaphore_wait(barrier, count - 1)
     mixed = []
-    for i in range(rows):
-        hidden = jnp.dot(
-            matrix1, shifted[pl.ds(i * block, 3 * block), :], preferred_element_type=jnp.float32
-        )
-        hidden = jnp.maximum(hidden + bias1, 0.0).astype(jnp.bfloat16)
-        mixed.append(jnp.dot(matrix2, hidden, preferred_element_type=jnp.float32))
-
     each = rows // count
     for target in range(count):
+        for i in range(len(mixed), min((target + 1) * each + 1, rows)):
+            hidden = jnp.dot(
+                matrix1, shifted[pl.ds(i * block, 3 * block), :], preferred_element_type=jnp.float32
+            )
+            hidden = jnp.maximum(hidden + bias1, 0.0).astype(jnp.bfloat16)
+            mixed.append(jnp.dot(matrix2, hidden, preferred_element_type=jnp.float32))
         totals = []
         for i in range(target * each, (target + 1) * each):
             summed = mixed[i][size : 2 * size]
@@ -229,20 +239,11 @@
             totals.append(total)
         result[target] = jnp.concatenate(totals, axis=0)
 
-    pl.semaphore_wait(barrier, count - 1)
-
-    def transfer(source, target):
-        return pltpu.make_async_remote_copy(
-            src_ref=result.at[target],
-            dst_ref=received.at[source],
-            send_sem=send_sem.at[target],
-            recv_sem=recv_sem.at[source],
-            device_id={"qrow": target},
-            device_id_type=pl.DeviceIdType.MESH,
-        )
-
-    for step in range(1, count):
-        transfer(me, lax.rem(me + step, count)).start()
+        @pl.when(target != me)
+        def _():
+            transfer(me, target).start()
+
+
     received[me] = result[me]
     for step in range(1, count):
         transfer(lax.rem(me + step, count), me).wait_recv()

time: 11.7 us -> 11.1 us (0.949)
  Pallas kernels: 10.3 us -> 9.67 us
    pallas_call x1, Pallas kernels: 10.3 us -> 9.67 us  [on_device(): pl.pallas_call(functools.partial(kernel, count, width, side), out_shape=p...]
where the time goes in v3:
time: 11.1 us; the launch traced here: 11 us
  Pallas kernels  9.67 us (87%)
  between operations  0.66 us (6%)
  other arithmetic  0.63 us (6%)
    pallas_call x1, Pallas kernels, on_device(): pl.pallas_call(functools.partial(kernel, count, width, side), out_shape=p...  9.67 us
    reshape x1, other arithmetic, on_device(): jnp.maximum(result + conv2_bias[0], 0.0)  0.63 us

profile of v3, /device:TPU:0, one launch (start us, length us, event | category | flops | bytes accessed | tf_op | source)
XLA Modules:
  0.0 11.0 jit_solution(2454396204887675245)
XLA Ops:
  0.7 9.7 %verify.1 = f32[3,16,256]{2,1,0:T(8,128)S(1)} custom-call(s32[3]{0:T(128)} %owner_hbm.1, f32[16]{0:T(128)} %bias1_hbm.1, bf16[64,1024]{1,0:T(8,128)(2,1)} %bitcast.15, bf16[256,1024]{1,0:T(8,128)(2,1)} %bitcast.14, bf16[27,3,16]{2,1,0:T(4,128)(2,1)} %bitcast.16, bf16[27,3,16]{2,1,0:T(4,128)(2,1)} %bitcast.17), custom_call_target="tpu_custom_call" | custom-call | tf_op jit(solution)/shard_map/verify/pallas_call | solution.py:268
  10.3 0.6 %maximum_bitcast_fusion = f32[3,1,2,8,256]{4,3,2,1,0:T(8,128)} fusion(f32[3,16,256]{2,1,0:T(8,128)S(1)} %verify.1, f32[]{:T(128)} %bitcast.13), kind=kLoop, calls=%fused_computation | loop fusion | flops 24576 | bytes 98308 | tf_op jit(solution)/shard_map/reshape | solution.py:304

commit v4 on v3

--- a/solution.py
+++ b/solution.py
@@ -96,6 +96,7 @@
     side,
     owner_hbm,
     bias1_hbm,
+    bias2_ref,
     query_hbm,
     map_hbm,
     weight1_hbm,
@@ -123,10 +124,10 @@
         pltpu.make_async_copy(source, target, load_sem.at[index])
         for index, (source, target) in enumerate(
             (
+                (map_hbm, map_ref),
+                (query_hbm, query_ref),
                 (weight1_hbm, weight1_ref),
                 (weight2_hbm, weight2_ref),
-                (map_hbm, map_ref),
-                (query_hbm, query_ref),
                 (bias1_hbm, bias1_ref),
                 (owner_hbm, owner_ref),
             )
@@ -170,8 +171,6 @@
     ) * (1.0 / math.sqrt(query_ref.shape[1]))
     scores = jnp.maximum(corr, 0.0)
     col_scale = 1.0 / (jnp.max(scores, axis=0, keepdims=True) + epsilon)
-    row_scale = 1.0 / (jnp.max(scores, axis=1, keepdims=True) + epsilon)
-    mutual = scores * (scores * col_scale) * (scores * row_scale)
 
     lane = lax.broadcasted_iota(jnp.int32, (1, positions), 1)
     column = lane & (side - 1)
@@ -189,13 +188,19 @@
         edge = lane < side if c == 0 else lane >= positions - side
         return jnp.where(edge, 0.0, moved)
 
-    along = [inner(mutual, d) for d in range(3)]
-    taps = [outer(along[d], c) for c in range(3) for d in range(3)]
     gap = jnp.zeros((width, positions), jnp.float32)
-    for i in range(rows):
-        shifted[pl.ds((i + 1) * block, block), :] = jnp.concatenate(
-            [tap[i * width : (i + 1) * width] for tap in taps] + [gap], axis=0
-        ).astype(jnp.bfloat16)
+
+    def place(first, last):
+        part = scores[first * width : last * width]
+        row_scale = 1.0 / (jnp.max(part, axis=1, keepdims=True) + epsilon)
+        mutual = part * (part * col_scale) * (part * row_scale)
+        along = [inner(mutual, d) for d in range(3)]
+        taps = [outer(along[d], c) for c in range(3) for d in range(3)]
+        for i in range(first, last):
+            start = (i - first) * width
+            shifted[pl.ds((i + 1) * block, block), :] = jnp.concatenate(
+                [tap[start : start + width] for tap in taps] + [gap], axis=0
+            ).astype(jnp.bfloat16)
 
     bias1 = jnp.concatenate(
         [jnp.full((width, positions), bias1_ref[o], jnp.float32) for o in range(channels)], axis=0
@@ -212,8 +217,13 @@
 
     pl.semaphore_wait(barrier, count - 1)
     mixed = []
+    placed = 0
     each = rows // count
     for target in range(count):
+        needed = min((target + 1) * each + 2, rows)
+        if needed > placed:
+            place(placed, needed)
+            placed = needed
         for i in range(len(mixed), min((target + 1) * each + 1, rows)):
             hidden = jnp.dot(
                 matrix1, shifted[pl.ds(i * block, 3 * block), :], preferred_element_type=jnp.float32
@@ -236,8 +246,8 @@
                     row = term if row is None else row + term
                 row = outer(row, c)
                 total = row if total is None else total + row
-            totals.append(total)
-        result[target] = jnp.concatenate(totals, axis=0)
+            totals.append(jnp.maximum(total + bias2_ref[0], 0.0))
+        result[target] = jnp.concatenate(totals, axis=0).astype(jnp.bfloat16)
 
         @pl.when(target != me)
         def _():
@@ -248,7 +258,7 @@
     for step in range(1, count):
         transfer(lax.rem(me + step, count), me).wait_recv()
     for r in range(out_ref.shape[0]):
-        out_ref[r] = received[owner_ref[r]]
+        out_ref[r] = received[owner_ref[r]].astype(jnp.float32)
     for step in range(1, count):
         transfer(me, lax.rem(me + step, count)).wait_send()
 
@@ -268,7 +278,9 @@
     result = pl.pallas_call(
         functools.partial(kernel, count, width, side),
         out_shape=pltpu.VMEM((rounds, each * width, positions), jnp.float32),
-        in_specs=[pl.BlockSpec(memory_space=pltpu.HBM)] * 6,
+        in_specs=[pl.BlockSpec(memory_space=pltpu.HBM)] * 2
+        + [pl.BlockSpec(memory_space=pltpu.SMEM)]
+        + [pl.BlockSpec(memory_space=pltpu.HBM)] * 4,
         out_specs=pl.BlockSpec(memory_space=pltpu.VMEM),
         scratch_shapes=[
             pltpu.SMEM((rounds,), jnp.int32),
@@ -283,8 +295,8 @@
             pltpu.VMEM((3, channels, LANE_STEP), jnp.float32),
             pltpu.VMEM((GROUPS * STRIDE, channels * width), jnp.float32),
             pltpu.VMEM(((rows + 2) * block, positions), jnp.bfloat16),
-            pltpu.VMEM((count, each * width, positions), jnp.float32),
-            pltpu.VMEM((count, each * width, positions), jnp.float32),
+            pltpu.VMEM((count, each * width, positions), jnp.bfloat16),
+            pltpu.VMEM((count, each * width, positions), jnp.bfloat16),
             pltpu.SemaphoreType.DMA((6,)),
             pltpu.SemaphoreType.DMA((count,)),
             pltpu.SemaphoreType.DMA((count,)),
@@ -296,12 +308,13 @@
     )(
         round_owner,
         conv1_bias,
+        conv2_bias,
         queries.reshape(maps * rows * width, depth),
         db_maps.reshape(positions, depth),
         taps_first(conv1_weight),
         taps_first(conv2_weight),
     )
-    return jnp.maximum(result + conv2_bias[0], 0.0).reshape(rounds, 1, each, width, positions)
+    return result.reshape(rounds, 1, each, width, positions)
 
 
 def solution(mesh):

time: 11.1 us -> 11 us (level)
  other arithmetic: 0.63 us -> 0 us
  local copies, waits for them, and re-layouts: 0 us -> 0.62 us
  Pallas kernels: 9.67 us -> 9.53 us
    reshape x1 -> x0, other arithmetic: 0.63 us -> none  [on_device(): jnp.maximum(result + conv2_bias[0], 0.0)]
    unnamed x0 -> x1, local copies, waits for them, and re-layouts: none -> 0.62 us
    pallas_call x1, Pallas kernels: 9.67 us -> 9.53 us  [on_device(): pl.pallas_call(functools.partial(kernel, count, width, side), out_shape=p...]
where the time goes in v4:
time: 11 us; the launch traced here: 10.8 us
  Pallas kernels  9.53 us (87%)
  between operations  0.66 us (6%)
  local copies, waits for them, and re-layouts  0.62 us (6%)
    pallas_call x1, Pallas kernels, on_device(): pl.pallas_call(functools.partial(kernel, count, width, side), out_shape=p...  9.53 us
    unnamed x1, local copies, waits for them, and re-layouts  0.62 us

profile of v4, /device:TPU:0, one launch (start us, length us, event | category | flops | bytes accessed | tf_op | source)
XLA Modules:
  0.0 10.8 jit_solution(13592334352760167105)
XLA Ops:
  0.7 9.5 %verify.1 = f32[3,16,256]{2,1,0:T(8,128)S(1)} custom-call(s32[3]{0:T(128)} %owner_hbm.1, f32[16]{0:T(128)} %bias1_hbm.1, f32[1]{0:T(128)S(6)} %copy.11.bias2_ref, bf16[64,1024]{1,0:T(8,128)(2,1)} %bitcast.13, bf16[256,1024]{1,0:T(8,128)(2,1)} %bitcast.12, bf16[27,3,16]{2,1,0:T(4,128)(2,1)} %bitcast.14, bf16[27,3,16]{2,1,0:T(4,128)(2,1)} %bitcast.15), custom_call_target="tpu_custom_call" | custom-call | tf_op jit(solution)/shard_map/verify/pallas_call | solution.py:278
  10.2 0.6 %copy.10 = f32[3,1,2,8,256]{4,3,2,1,0:T(8,128)} copy(f32[3,1,2,8,256]{4,3,2,1,0:T(8,128)S(1)} %bitcast.11) | data formatting | bytes 98304

commit v5 on v3

--- a/solution.py
+++ b/solution.py
@@ -33,39 +33,7 @@
     return value
 
 
-def fill_picks(width, pick_ref):
-    rows = GROUPS * STRIDE
-    block = SLOTS * width
-    lane = lax.broadcasted_iota(jnp.int32, (1, LANE_STEP), 1)
-    a = sum((lane >= k * block).astype(jnp.int32) for k in (1, 2))
-    offset = lane - a * block
-    tap = sum((offset >= k * width).astype(jnp.int32) for k in range(1, SLOTS))
-    c = (tap >= 3).astype(jnp.int32) + (tap >= 6).astype(jnp.int32)
-    d = tap - 3 * c
-    valid = (tap < TAPS) & (lane < 3 * block)
-    base = jnp.where(valid, tap_row(a, 0, c, d), -2 * rows)
-    row = lax.broadcasted_iota(jnp.int32, (rows, LANE_STEP), 0)
-    for b in range(3):
-        pick_ref[b] = jnp.where(row == base + tap_row(0, b, 0, 0), 1.0, 0.0).astype(jnp.bfloat16)
-    return offset - tap * width - lax.broadcasted_iota(jnp.int32, (width, LANE_STEP), 0) + 1
-
-
-def first_matrix(taps, width, pick_ref, band, chosen_ref):
-    for b in range(3):
-        chosen_ref[b] = lax.dot_general(
-            taps, pick_ref[b], (((0,), (0,)), ((), ())), preferred_element_type=jnp.float32
-        )
-    masks = [band == b for b in range(3)]
-    return jnp.concatenate(
-        [
-            banded(masks, [chosen_ref[b, pl.ds(o, 1), :] for b in range(3)])
-            for o in range(taps.shape[1])
-        ],
-        axis=0,
-    ).astype(jnp.bfloat16)[:, : 3 * SLOTS * width]
-
-
-def second_matrix(taps, width, wide_ref):
+def band_rows(taps, width, wide_ref, backward, slots):
     channels = taps.shape[1]
     lanes = channels * width
     lane = lax.broadcasted_iota(jnp.int32, (channels, lanes), 1)
@@ -77,17 +45,18 @@
         for k in range(1, channels)
     )
     column = lax.broadcasted_iota(jnp.int32, (1, lanes), 1) - channel * width
-    band = column - lax.broadcasted_iota(jnp.int32, (width, lanes), 0) + 1
-    masks = [band == b for b in range(3)]
-    return jnp.concatenate(
-        [
-            banded(masks, [wide_ref[pl.ds(tap_row(a, b, c, d), 1), :] for b in range(3)])
-            for a in range(3)
-            for c in range(3)
-            for d in range(3)
-        ],
-        axis=0,
-    ).astype(jnp.bfloat16)
+    band = column - lax.broadcasted_iota(jnp.int32, (width, lanes), 0)
+    masks = [band == ((1 - b) if backward else (b - 1)) for b in range(3)]
+    pieces = []
+    for a in range(3):
+        for c in range(3):
+            for d in range(3):
+                pieces.append(
+                    banded(masks, [wide_ref[pl.ds(tap_row(a, b, c, d), 1), :] for b in range(3)])
+                )
+        if slots > TAPS:
+            pieces.append(jnp.zeros(((slots - TAPS) * width, lanes), jnp.float32))
+    return jnp.concatenate(pieces, axis=0)
 
 
 def kernel(
@@ -109,9 +78,8 @@
     weight2_ref,
     spread1,
     spread2,
-    pick,
-    chosen,
-    wide,
+    wide1,
+    wide2,
     shifted,
     result,
     received,
@@ -150,7 +118,6 @@
     block = SLOTS * width
     size = TAPS * width
 
-    band = fill_picks(width, pick)
     for spread in (spread1, spread2):
         spread[...] = jnp.zeros_like(spread)
     blank = jnp.zeros((block, positions), jnp.bfloat16)
@@ -159,8 +126,12 @@
     for load in loads:
         load.wait()
 
-    matrix1 = first_matrix(tap_matrix(weight1_ref, spread1), width, pick, band, chosen)
-    matrix2 = second_matrix(tap_matrix(weight2_ref, spread2), width, wide)
+    tall = band_rows(tap_matrix(weight1_ref, spread1), width, wide1, True, SLOTS)
+    spare = jnp.zeros((LANE_STEP - tall.shape[0], tall.shape[1]), jnp.float32)
+    matrix1 = jnp.concatenate([tall, spare], axis=0).T.astype(jnp.bfloat16)[:, : 3 * block]
+    matrix2 = band_rows(tap_matrix(weight2_ref, spread2), width, wide2, False, TAPS).astype(
+        jnp.bfloat16
+    )
 
     corr = lax.dot_general(
         query_ref[...],
@@ -279,8 +250,7 @@
             pltpu.VMEM((27, 3, channels), jnp.bfloat16),
             pltpu.VMEM((GROUPS, STRIDE, channels), jnp.float32),
             pltpu.VMEM((GROUPS, STRIDE, channels), jnp.float32),
-            pltpu.VMEM((3, GROUPS * STRIDE, LANE_STEP), jnp.bfloat16),
-            pltpu.VMEM((3, channels, LANE_STEP), jnp.float32),
+            pltpu.VMEM((GROUPS * STRIDE, channels * width), jnp.float32),
             pltpu.VMEM((GROUPS * STRIDE, channels * width), jnp.float32),
             pltpu.VMEM(((rows + 2) * block, positions), jnp.bfloat16),
             pltpu.VMEM((count, each * width, positions), jnp.float32),

time: 11.1 us -> 11.1 us (level)
  no operation moved by 1% of the time
where the time goes in v5:
time: 11.1 us; the launch traced here: 10.9 us
  Pallas kernels  9.63 us (87%)
  between operations  0.66 us (6%)
  other arithmetic  0.63 us (6%)
    pallas_call x1, Pallas kernels, on_device(): pl.pallas_call(functools.partial(kernel, count, width, side), out_shape=p...  9.63 us
    reshape x1, other arithmetic, on_device(): jnp.maximum(result + conv2_bias[0], 0.0)  0.63 us

profile of v5, /device:TPU:0, one launch (start us, length us, event | category | flops | bytes accessed | tf_op | source)
XLA Modules:
  0.0 10.9 jit_solution(10042508233689078400)
XLA Ops:
  0.7 9.6 %verify.1 = f32[3,16,256]{2,1,0:T(8,128)S(1)} custom-call(s32[3]{0:T(128)} %owner_hbm.1, f32[16]{0:T(128)} %bias1_hbm.1, bf16[64,1024]{1,0:T(8,128)(2,1)} %bitcast.15, bf16[256,1024]{1,0:T(8,128)(2,1)} %bitcast.14, bf16[27,3,16]{2,1,0:T(4,128)(2,1)} %bitcast.16, bf16[27,3,16]{2,1,0:T(4,128)(2,1)} %bitcast.17), custom_call_target="tpu_custom_call" | custom-call | tf_op jit(solution)/shard_map/verify/pallas_call | solution.py:239
  10.3 0.6 %maximum_bitcast_fusion = f32[3,1,2,8,256]{4,3,2,1,0:T(8,128)} fusion(f32[3,16,256]{2,1,0:T(8,128)S(1)} %verify.1, f32[]{:T(128)} %bitcast.13), kind=kLoop, calls=%fused_computation | loop fusion | flops 24576 | bytes 98308 | tf_op jit(solution)/shard_map/reshape | solution.py:274

commit v6 on v5

--- a/solution.py
+++ b/solution.py
@@ -134,12 +134,12 @@
     )
 
     corr = lax.dot_general(
+        map_ref[...],
         query_ref[...],
-        map_ref[...],
         (((1,), (1,)), ((), ())),
         preferred_element_type=jnp.float32,
     ) * (1.0 / math.sqrt(query_ref.shape[1]))
-    scores = jnp.maximum(corr, 0.0)
+    scores = jnp.maximum(corr.T, 0.0)
     col_scale = 1.0 / (jnp.max(scores, axis=0, keepdims=True) + epsilon)
     row_scale = 1.0 / (jnp.max(scores, axis=1, keepdims=True) + epsilon)
     mutual = scores * (scores * col_scale) * (scores * row_scale)

time: 11.1 us -> 11.1 us (level)
  no operation moved by 1% of the time
where the time goes in v6:
time: 11.1 us; the launch traced here: 11 us
  Pallas kernels  9.71 us (87%)
  between operations  0.66 us (6%)
  other arithmetic  0.63 us (6%)
    pallas_call x1, Pallas kernels, on_device(): pl.pallas_call(functools.partial(kernel, count, width, side), out_shape=p...  9.71 us
    reshape x1, other arithmetic, on_device(): jnp.maximum(result + conv2_bias[0], 0.0)  0.63 us

profile of v6, /device:TPU:0, one launch (start us, length us, event | category | flops | bytes accessed | tf_op | source)
XLA Modules:
  0.0 11.0 jit_solution(9964803604682085539)
XLA Ops:
  0.7 9.7 %verify.1 = f32[3,16,256]{2,1,0:T(8,128)S(1)} custom-call(s32[3]{0:T(128)} %owner_hbm.1, f32[16]{0:T(128)} %bias1_hbm.1, bf16[64,1024]{1,0:T(8,128)(2,1)} %bitcast.15, bf16[256,1024]{1,0:T(8,128)(2,1)} %bitcast.14, bf16[27,3,16]{2,1,0:T(4,128)(2,1)} %bitcast.16, bf16[27,3,16]{2,1,0:T(4,128)(2,1)} %bitcast.17), custom_call_target="tpu_custom_call" | custom-call | tf_op jit(solution)/shard_map/verify/pallas_call | solution.py:239
  10.4 0.6 %maximum_bitcast_fusion = f32[3,1,2,8,256]{4,3,2,1,0:T(8,128)} fusion(f32[3,16,256]{2,1,0:T(8,128)S(1)} %verify.1, f32[]{:T(128)} %bitcast.13), kind=kLoop, calls=%fused_computation | loop fusion | flops 24576 | bytes 98308 | tf_op jit(solution)/shard_map/reshape | solution.py:274

commit v7 on v5

--- a/solution.py
+++ b/solution.py
@@ -91,10 +91,10 @@
         pltpu.make_async_copy(source, target, load_sem.at[index])
         for index, (source, target) in enumerate(
             (
+                (map_hbm, map_ref),
+                (query_hbm, query_ref),
                 (weight1_hbm, weight1_ref),
                 (weight2_hbm, weight2_ref),
-                (map_hbm, map_ref),
-                (query_hbm, query_ref),
                 (bias1_hbm, bias1_ref),
                 (owner_hbm, owner_ref),
             )
@@ -141,8 +141,6 @@
     ) * (1.0 / math.sqrt(query_ref.shape[1]))
     scores = jnp.maximum(corr, 0.0)
     col_scale = 1.0 / (jnp.max(scores, axis=0, keepdims=True) + epsilon)
-    row_scale = 1.0 / (jnp.max(scores, axis=1, keepdims=True) + epsilon)
-    mutual = scores * (scores * col_scale) * (scores * row_scale)
 
     lane = lax.broadcasted_iota(jnp.int32, (1, positions), 1)
     column = lane & (side - 1)
@@ -160,13 +158,19 @@
         edge = lane < side if c == 0 else lane >= positions - side
         return jnp.where(edge, 0.0, moved)
 
-    along = [inner(mutual, d) for d in range(3)]
-    taps = [outer(along[d], c) for c in range(3) for d in range(3)]
     gap = jnp.zeros((width, positions), jnp.float32)
-    for i in range(rows):
-        shifted[pl.ds((i + 1) * block, block), :] = jnp.concatenate(
-            [tap[i * width : (i + 1) * width] for tap in taps] + [gap], axis=0
-        ).astype(jnp.bfloat16)
+
+    def place(first, last):
+        part = scores[first * width : last * width]
+        row_scale = 1.0 / (jnp.max(part, axis=1, keepdims=True) + epsilon)
+        mutual = part * (part * col_scale) * (part * row_scale)
+        along = [inner(mutual, d) for d in range(3)]
+        taps = [outer(along[d], c) for c in range(3) for d in range(3)]
+        for i in range(first, last):
+            start = (i - first) * width
+            shifted[pl.ds((i + 1) * block, block), :] = jnp.concatenate(
+                [tap[start : start + width] for tap in taps] + [gap], axis=0
+            ).astype(jnp.bfloat16)
 
     bias1 = jnp.concatenate(
         [jnp.full((width, positions), bias1_ref[o], jnp.float32) for o in range(channels)], axis=0
@@ -183,8 +187,13 @@
 
     pl.semaphore_wait(barrier, count - 1)
     mixed = []
+    placed = 0
     each = rows // count
     for target in range(count):
+        needed = min((target + 1) * each + 2, rows)
+        if needed > placed:
+            place(placed, needed)
+            placed = needed
         for i in range(len(mixed), min((target + 1) * each + 1, rows)):
             hidden = jnp.dot(
                 matrix1, shifted[pl.ds(i * block, 3 * block), :], preferred_element_type=jnp.float32

time: 11.1 us -> 11 us (level)
  no operation moved by 1% of the time
where the time goes in v7:
time: 11 us; the launch traced here: 10.9 us
  Pallas kernels  9.58 us (87%)
  between operations  0.66 us (6%)
  other arithmetic  0.63 us (6%)
    pallas_call x1, Pallas kernels, on_device(): pl.pallas_call(functools.partial(kernel, count, width, side), out_shape=p...  9.58 us
    reshape x1, other arithmetic, on_device(): jnp.maximum(result + conv2_bias[0], 0.0)  0.63 us

profile of v7, /device:TPU:0, one launch (start us, length us, event | category | flops | bytes accessed | tf_op | source)
XLA Modules:
  0.0 10.9 jit_solution(12314339833527610556)
XLA Ops:
  0.7 9.6 %verify.1 = f32[3,16,256]{2,1,0:T(8,128)S(1)} custom-call(s32[3]{0:T(128)} %owner_hbm.1, f32[16]{0:T(128)} %bias1_hbm.1, bf16[64,1024]{1,0:T(8,128)(2,1)} %bitcast.15, bf16[256,1024]{1,0:T(8,128)(2,1)} %bitcast.14, bf16[27,3,16]{2,1,0:T(4,128)(2,1)} %bitcast.16, bf16[27,3,16]{2,1,0:T(4,128)(2,1)} %bitcast.17), custom_call_target="tpu_custom_call" | custom-call | tf_op jit(solution)/shard_map/verify/pallas_call | solution.py:248
  10.2 0.6 %maximum_bitcast_fusion = f32[3,1,2,8,256]{4,3,2,1,0:T(8,128)} fusion(f32[3,16,256]{2,1,0:T(8,128)S(1)} %verify.1, f32[]{:T(128)} %bitcast.13), kind=kLoop, calls=%fused_computation | loop fusion | flops 24576 | bytes 98308 | tf_op jit(solution)/shard_map/reshape | solution.py:283
